TPU v7x, 256 devices: a whole 4x4x8 slice. The times are simulated.
256 devices in a mesh: dp: 16 (over z_hi, x), seq: 16 (over z_lo, y, core).
Axes of the slice: x: 4, y: 4, z: 8 (z_hi: 4, z_lo: 2; z = z_hi * 2 + z_lo), core: 2. Of those that a mesh axis runs over, the one named last changes fastest.
Arguments:
- inputs: bfloat16 [4096, 5120], P('seq', 'dp'), may hold values from -24 to 24
- tangents: bfloat16 [4096, 5120], P('seq', 'dp'), may hold values from -6 to 6
- query_weight: bfloat16 [5120, 4096], P('dp', 'seq'), may hold values from -1 to 1
- key_weight: bfloat16 [5120, 4096], P('dp', 'seq'), may hold values from -1 to 1
- value_weight: bfloat16 [5120, 4096], P('dp', 'seq'), may hold values from -0.078125 to 0.078125
- query_gain: float32 [4096], P('seq'), may hold values from 0.5 to 5.5
- key_gain: float32 [4096], P('seq'), may hold values from 0.5 to 5.5
- out_weight: bfloat16 [4096, 5120], P('seq', 'dp'), may hold values from -0.09375 to 0.09375
Outputs:
- attended: bfloat16 [4096, 5120], P('dp', 'seq')
- attended_tangent: bfloat16 [4096, 5120], P('dp', 'seq')
All inputs are finite; a program needn't handle non-finite values.
Results may differ from a plain program's by a relative error of at most 0.035.
Values may be sent and summed in bfloat16 or wider, within the bound.
A program may use at most 128 MiB of HBM per device.

v0:
```python
import jax
import jax.numpy as jnp
from jax import lax
from jax.sharding import PartitionSpec as P

HD = 128


def head_norm(raw, raw_tan, gain):
    rows = raw.shape[0]
    heads = gain.shape[0] // HD
    raw = raw.reshape(rows, heads, HD)
    raw_tan = raw_tan.reshape(rows, heads, HD)
    gain = gain.reshape(heads, HD)
    ms = jnp.mean(raw * raw, axis=-1, keepdims=True)
    inv = lax.rsqrt(ms + 1e-06)
    inner = jnp.mean(raw * raw_tan, axis=-1, keepdims=True)
    normed = gain * raw * inv
    normed_tan = gain * inv * (raw_tan - raw * inner * inv * inv)
    return (normed.astype(jnp.bfloat16), normed_tan.astype(jnp.bfloat16))


def attend(query, query_tan, keys, keys_tan, values, values_tan):
    scale = 1.0 / jnp.sqrt(jnp.float32(HD))
    scores = jnp.einsum("qhd,khd->hqk", query, keys, preferred_element_type=jnp.float32) * scale
    scores_tan = (
        jnp.einsum("qhd,khd->hqk", query_tan, keys, preferred_element_type=jnp.float32)
        + jnp.einsum("qhd,khd->hqk", query, keys_tan, preferred_element_type=jnp.float32)
    ) * scale
    top = jnp.max(scores, axis=-1, keepdims=True)
    expo = jnp.exp(scores - top)
    probs = expo / jnp.sum(expo, axis=-1, keepdims=True)
    probs_tan = probs * (scores_tan - jnp.sum(probs * scores_tan, axis=-1, keepdims=True))
    probs_b = probs.astype(jnp.bfloat16)
    probs_tan_b = probs_tan.astype(jnp.bfloat16)
    heads_out = jnp.einsum("hqk,khd->qhd", probs_b, values, preferred_element_type=jnp.float32)
    heads_tan = jnp.einsum(
        "hqk,khd->qhd", probs_tan_b, values, preferred_element_type=jnp.float32
    ) + jnp.einsum("hqk,khd->qhd", probs_b, values_tan, preferred_element_type=jnp.float32)
    rows = heads_out.shape[0]
    return (
        heads_out.astype(jnp.bfloat16).reshape(rows, -1),
        heads_tan.astype(jnp.bfloat16).reshape(rows, -1),
    )


def shards(
    inputs, tangents, query_weight, key_weight, value_weight, query_gain, key_gain, out_weight
):
    width = query_weight.shape[1]
    heads = width // HD
    whole, whole_tan = (
        lax.all_gather(inputs, "seq", axis=0, tiled=True),
        lax.all_gather(tangents, "seq", axis=0, tiled=True),
    )
    local_rows = whole.shape[0] // lax.axis_size("dp")
    all_weights = jnp.concatenate([query_weight, key_weight, value_weight], axis=1)
    sums = lax.psum_scatter(
        jnp.concatenate(
            [
                jnp.dot(whole, all_weights, preferred_element_type=jnp.float32),
                jnp.dot(whole_tan, all_weights, preferred_element_type=jnp.float32),
            ],
            axis=1,
        ).astype(jnp.bfloat16),
        "dp",
        scatter_dimension=0,
        tiled=True,
    ).astype(jnp.float32)
    query, query_tan = head_norm(sums[:, :width], sums[:, 3 * width : 4 * width], query_gain)
    key_own, key_own_tan = head_norm(
        sums[:, width : 2 * width], sums[:, 4 * width : 5 * width], key_gain
    )
    value_own = sums[:, 2 * width : 3 * width].astype(jnp.bfloat16).reshape(local_rows, heads, HD)
    value_own_tan = sums[:, 5 * width :].astype(jnp.bfloat16).reshape(local_rows, heads, HD)
    stacked = jnp.stack([key_own, key_own_tan, value_own, value_own_tan])
    gathered = lax.all_gather(stacked, "dp", axis=1, tiled=True)
    keys, keys_tan, values, values_tan = (gathered[0], gathered[1], gathered[2], gathered[3])
    heads_out, heads_tan = attend(query, query_tan, keys, keys_tan, values, values_tan)
    both_heads = jnp.concatenate([heads_out, heads_tan], axis=0)
    terms = jnp.dot(
        both_heads,
        lax.all_gather(out_weight, "dp", axis=1, tiled=True),
        preferred_element_type=jnp.float32,
    )
    summed = lax.psum_scatter(
        terms.astype(jnp.bfloat16), "seq", scatter_dimension=1, tiled=True
    ).astype(jnp.float32)
    return (summed[:local_rows].astype(jnp.bfloat16), summed[local_rows:].astype(jnp.bfloat16))


def solution(mesh):
    in_specs = (
        P("seq", "dp"),
        P("seq", "dp"),
        P("dp", "seq"),
        P("dp", "seq"),
        P("dp", "seq"),
        P("seq"),
        P("seq"),
        P("seq", "dp"),
    )
    out_specs = (P("dp", "seq"), P("dp", "seq"))
    return jax.shard_map(shards, mesh=mesh, in_specs=in_specs, out_specs=out_specs, check_vma=False)
```

profile of v0, /device:TPU:1, one launch (start us, length us, event | category | flops | bytes accessed | tf_op | source)
XLA Modules:
  0.0 540.8 jit_solution(15682085707928954902)
XLA Ops:
  7.2 0.0 all-gather.5.cloned.1.call-start
  7.2 0.7 all-gather.5.cloned.1.call-update
  7.9 0.0 all-gather.7.cloned.1.call-start
  7.9 0.7 all-gather.7.cloned.1.call-update
  8.6 0.0 reduce-scatter.3.cloned.1.call-start
  8.7 0.9 constant_dynamic-update-slice_fusion.2
  9.6 0.9 constant_dynamic-update-slice_fusion.1
  10.6 0.9 constant_dynamic-update-slice_fusion
  11.5 44.6 %all-gather.5.cloned.1.call-done = bf16[4096,320]{0,1:T(8,128)(2,1)} async-done(((bf16[256,320]{0,1:T(8,128)(2,1)}), bf16[4096,320]{0,1:T(8,128)(2,1)}) %all-gather.5.cloned.1.call-update) | async-done | bytes 2621456 | tf_op jit(solution)/shard_map/all_gather | solution.py:53
  56.1 7.1 %fusion.2 = bf16[4096,768]{0,1:T(8,128)(2,1)} fusion(bf16[320,768]{1,0:T(8,128)(2,1)S(1)} %constant_dynamic-update-slice_fusion, bf16[4096,320]{0,1:T(8,128)(2,1)} %all-gather.5.cloned.1.call-done), kind=kOutput, calls=%fused_computation.11 | convolution fusion | flops 2016411648 | bytes 9404416 | tf_op jit(solution)/shard_map/dot_general | solution.py:61
  63.2 36.6 %all-gather.7.cloned.1.call-done = bf16[4096,320]{0,1:T(8,128)(2,1)} async-done(((bf16[256,320]{0,1:T(8,128)(2,1)}), bf16[4096,320]{0,1:T(8,128)(2,1)}) %all-gather.7.cloned.1.call-update) | async-done | bytes 2621456 | tf_op jit(solution)/shard_map/all_gather | solution.py:54
  99.8 5.6 %fusion.3 = bf16[4096,768]{0,1:T(8,128)(2,1)S(1)} fusion(bf16[320,768]{1,0:T(8,128)(2,1)S(1)} %constant_dynamic-update-slice_fusion, bf16[4096,320]{0,1:T(8,128)(2,1)} %all-gather.7.cloned.1.call-done), kind=kOutput, calls=%fused_computation.12 | convolution fusion | flops 2016411648 | bytes 9404416 | tf_op jit(solution)/shard_map/dot_general | solution.py:62
  105.4 11.4 %pad_maximum_fusion = bf16[4096,1536]{0,1:T(8,128)(2,1)} fusion(bf16[4096,768]{0,1:T(8,128)(2,1)S(1)} %fusion.3, bf16[4096,768]{0,1:T(8,128)(2,1)S(1)} %copy-done), kind=kLoop, calls=%fused_computation.1 | loop fusion | flops 25165824 | bytes 25165824 | tf_op jit(solution)/shard_map/concatenate | solution.py:59
  116.8 0.0 reduce-scatter.3.cloned.1.call-update
  116.9 0.0 copy-start.1
  116.9 0.0 all-gather.9.cloned.1.call-start
  116.9 159.5 %reduce-scatter.3.cloned.1.call-done = bf16[256,1536]{0,1:T(8,128)(2,1)} async-done(((bf16[4096,1536]{0,1:T(8,128)(2,1)}), bf16[256,1536]{0,1:T(8,128)(2,1)}) %reduce-scatter.3.cloned.1.call-update) | async-done | bytes 786448 | tf_op jit(solution)/shard_map/reduce_scatter | solution.py:58
  276.4 1.2 convert_element_type.56
  277.7 0.1 multiply_reduce_fusion.2
  277.8 1.2 fusion.38
  279.0 0.1 copy.10
  279.1 0.1 copy.12
  279.2 1.0 fusion.39
  280.2 0.1 copy.13
  280.4 0.1 copy.14
  280.5 0.0 copy-done.2
  280.5 0.2 multiply_convert_fusion.9
  280.7 0.9 pad_maximum_fusion.1
  281.6 0.0 all-gather.9.cloned.1.call-update
  281.7 0.0 all-gather.11.cloned.1.call-start
  281.7 0.5 all-gather.11.cloned.1.call-update
  282.3 0.2 reduce-scatter.5.cloned.1.call-start
  282.5 0.1 copy.15
  282.6 0.1 copy.18
  282.8 0.1 multiply_convert_fusion.7
  282.9 100.7 %all-gather.9.cloned.1.call-done = bf16[4,4096,2,128]{3,1,2,0:T(8,128)(2,1)} async-done(((bf16[4,256,2,128]{3,1,2,0:T(8,128)(2,1)}), bf16[4,4096,2,128]{3,1,2,0:T(8,128)(2,1)}) %all-gather.9.cloned.1.call-update) | async-done | bytes 8388624 | tf_op jit(solution)/shard_map/all_gather | solution.py:77
  383.6 7.4 %fusion.41 = (f32[2,256]{1,0:T(2,128)S(1)}, f32[2,256,4096]{2,1,0:T(8,128)}) fusion(bf16[256,2,128]{2,0,1:T(8,128)(2,1)S(1)} %multiply_convert_fusion.7, bf16[4,4096,2,128]{3,1,2,0:T(8,128)(2,1)} %all-gather.9.cloned.1.call-done), kind=kOutput, calls=%fused_computation.58 | convolution fusion | flops 543166464 | bytes 10618880 | tf_op jit(solution)/shard_map/sub | solution.py:31
  391.0 5.5 %fusion.15 = bf16[2,128,256]{2,1,0:T(8,128)(2,1)S(1)} fusion(bf16[4,4096,2,128]{3,1,2,0:T(8,128)(2,1)} %all-gather.9.cloned.1.call-done, f32[2,256]{1,0:T(2,128)S(1)} %get-tuple-element.16, bf16[256,2,128]{2,0,1:T(8,128)(2,1)S(1)} %multiply_convert_fusion.7), kind=kOutput, calls=%fused_computation.29 | convolution fusion | flops 1082200576 | bytes 4458496 | tf_op jit(solution)/shard_map/hqk,khd->qhd/dot_general | solution.py:36
  396.5 5.5 %fusion.7 = f32[2,128,256]{2,1,0:T(8,128)S(1)} fusion(bf16[4,4096,2,128]{3,1,2,0:T(8,128)(2,1)} %all-gather.9.cloned.1.call-done, f32[2,256]{1,0:T(2,128)S(1)} %get-tuple-element.16, bf16[256,2,128]{2,0,1:T(8,128)(2,1)S(1)} %multiply_convert_fusion.7), kind=kOutput, calls=%fused_computation.18 | convolution fusion | flops 1082135040 | bytes 4589568 | tf_op jit(solution)/shard_map/hqk,khd->qhd/dot_general | solution.py:39
  402.0 3.1 fusion.11
  405.1 0.9 copy-done.3
  406.1 6.2 %multiply_reduce_fusion = (f32[2,256]{1,0:T(2,128)S(1)}, f32[2,256,4096]{2,1,0:T(8,128)}) fusion(f32[2,256,4096]{2,1,0:T(8,128)S(1)} %copy-done.3, f32[2,256]{1,0:T(2,128)S(1)} %get-tuple-element.16, f32[2,256,4096]{2,1,0:T(8,128)S(1)} %fusion.11, bf16[256,2,128]{2,0,1:T(8,128)(2,1)S(1)} %multiply_convert_fusion.7, ...), kind=kOutput, calls=%fused_computation.3 | convolution fusion | flops 547356160 | bytes 27398144 | tf_op jit(solution)/shard_map/qhd,khd->hqk/dot_general | solution.py:28
  412.3 8.6 %fusion.14 = bf16[2,128,256]{2,1,0:T(8,128)(2,1)S(1)} fusion(f32[2,128,256]{2,1,0:T(8,128)S(1)} %fusion.7, f32[2,256,4096]{2,1,0:T(8,128)} %get-tuple-element.19, f32[2,256]{1,0:T(2,128)S(1)} %get-tuple-element.18, bf16[4,4096,2,128]{3,1,2,0:T(8,128)(2,1)} %all-gather.9.cloned.1.call-done, f32[2,256]{1,0:T(2,128)S(1)} %get-tuple-element.16, ...), kind=kOutput, calls=%fused_computation.28 | convolution fusion | flops 1086460416 | bytes 13111296 | tf_op jit(solution)/shard_map/hqk,khd->qhd/dot_general | solution.py:37
  420.9 39.6 %all-gather.11.cloned.1.call-done = bf16[256,5120]{0,1:T(8,128)(2,1)} async-done(((bf16[256,320]{0,1:T(8,128)(2,1)}), bf16[256,5120]{0,1:T(8,128)(2,1)}) %all-gather.11.cloned.1.call-update) | async-done | bytes 2621456 | tf_op jit(solution)/shard_map/all_gather | solution.py:83
  460.5 5.6 %convolution_convert_fusion = bf16[512,5120]{0,1:T(8,128)(2,1)} fusion(bf16[256,5120]{0,1:T(8,128)(2,1)} %all-gather.11.cloned.1.call-done, bf16[256,256]{0,1:T(8,128)(2,1)S(1)} %bitcast.84, bf16[256,256]{0,1:T(8,128)(2,1)S(1)} %bitcast.83), kind=kOutput, calls=%fused_computation.8 | convolution fusion | flops 1345323008 | bytes 8126464 | tf_op jit(solution)/shard_map/dot_general | solution.py:81
  466.0 0.0 reduce-scatter.5.cloned.1.call-update
  466.1 66.2 %reduce-scatter.5.cloned.1.call-done = bf16[512,320]{0,1:T(8,128)(2,1)} async-done(((bf16[512,5120]{0,1:T(8,128)(2,1)}), bf16[512,320]{0,1:T(8,128)(2,1)}) %reduce-scatter.5.cloned.1.call-update) | async-done | bytes 327696 | tf_op jit(solution)/shard_map/reduce_scatter | solution.py:86
  532.3 1.7 fusion.40
  (7 shorter events, 0.0 us)
Async XLA Ops:
  7.2 48.9 %all-gather.5.cloned.1.call-start = ((), (), s32[]{:S(2)}) async-start(), calls=%async_computation.2 | async-start | bytes 2785280 | tf_op jit(solution)/shard_map/all_gather | solution.py:53
  7.9 91.9 %all-gather.7.cloned.1.call-start = ((), (), s32[]{:S(2)}) async-start(), calls=%async_computation.3 | async-start | bytes 2785280 | tf_op jit(solution)/shard_map/all_gather | solution.py:54
  8.6 267.8 %reduce-scatter.3.cloned.1.call-start = ((), (), s32[]{:S(2)}) async-start(), calls=%async_computation.4 | async-start | bytes 13369344 | tf_op jit(solution)/shard_map/reduce_scatter | solution.py:58
  99.8 5.6 %copy-start = (bf16[4096,768]{0,1:T(8,128)(2,1)S(1)}, bf16[4096,768]{0,1:T(8,128)(2,1)}, u32[]{:S(2)}) copy-start(bf16[4096,768]{0,1:T(8,128)(2,1)} %fusion.2) | copy-start | bytes 18874372
  116.8 163.7 %copy-start.2 = (f32[256]{0:T(256)S(1)}, f32[256]{0:T(256)}, u32[]{:S(2)}) copy-start(f32[256]{0:T(256)} %param.14) | copy-start | bytes 3076
  116.9 165.9 %copy-start.1 = (f32[256]{0:T(256)S(1)}, f32[256]{0:T(256)}, u32[]{:S(2)}) copy-start(f32[256]{0:T(256)} %param.13) | copy-start | bytes 3076
  116.9 266.7 %all-gather.9.cloned.1.call-start = ((), (), s32[]{:S(2)}) async-start(), calls=%async_computation.5 | async-start | bytes 8912896 | tf_op jit(solution)/shard_map/all_gather | solution.py:77
  281.7 178.8 %all-gather.11.cloned.1.call-start = ((), (), s32[]{:S(2)}) async-start(), calls=%async_computation.6 | async-start | bytes 2785280 | tf_op jit(solution)/shard_map/all_gather | solution.py:83
  282.3 250.0 %reduce-scatter.5.cloned.1.call-start = ((), (), s32[]{:S(2)}) async-start(), calls=%async_computation.7 | async-start | bytes 5570560 | tf_op jit(solution)/shard_map/reduce_scatter | solution.py:86
  402.0 4.0 copy-start.3
Sparse Core Ops, SparseCore 0:
  9.8 46.2 all-gather.4
  57.8 41.9 all-gather.6
  117.0 159.4 reduce-scatter.2
  281.8 101.7 all-gather.8
  385.9 74.5 all-gather.10
  466.2 66.0 reduce-scatter.4
where the time goes:
time: 544 us; the launch traced here: 541 us
  waiting for transfers between devices  449 us (83%)
  matrix products  54.6 us (10%)
  between operations  14.3 us (3%)
  other arithmetic  14 us (3%)
  local copies, waits for them, and re-layouts  8.39 us (2%)
    reduce_scatter x1, waiting for transfers between devices, shards(): lax.psum_scatter(jnp.concatenate([jnp.dot(whole, all_weights, preferred_e...  160 us
    all_gather x1, waiting for transfers between devices, shards(): gathered = lax.all_gather(stacked, 'dp', axis=1, tiled=True)  101 us
    reduce_scatter x1, waiting for transfers between devices, shards(): lax.psum_scatter(terms.astype(jnp.bfloat16), 'seq', scatter_dimension=1,...  66.2 us
    all_gather x1, waiting for transfers between devices, shards(): lax.all_gather(inputs, 'seq', axis=0, tiled=True)  44.6 us
    all_gather x1, waiting for transfers between devices, shards(): lax.all_gather(out_weight, 'dp', axis=1, tiled=True)  39.6 us
    all_gather x1, waiting for transfers between devices, shards(): lax.all_gather(tangents, 'seq', axis=0, tiled=True)  36.6 us
    concatenate x1, other arithmetic, shards(): jnp.concatenate([jnp.dot(whole, all_weights, preferred_element_type=jnp.f...  11.4 us
  transfers between devices with their start and end apart: 6, of which 6 were waited for; matrix products, arithmetic and copies ran while one was open for 9% of the time, Pallas kernels for 0%

commit v1 on v0

v1 whole, which is shorter than its diff:
```python
import jax
import jax.numpy as jnp
from jax import lax
from jax.experimental import pallas as pl
from jax.experimental.pallas import tpu as pltpu
from jax.sharding import PartitionSpec as P

HD = 128
F = 320
TB = 256
TOKENS = 4096
HALF = 128
BF16 = jnp.bfloat16
F32 = jnp.float32
N_SEMS = 192


def kernel(
    in_ref, tin_ref, wq_ref, wk_ref, wv_ref, gq_ref, gk_ref, wo_ref,
    out_ref,
    WB, GB, AB, AN, WOB, PART, SB, RB, HOLD, OWN, KB, VB, QB, S, ST, MX, LI, EB, UB, AO, AT, HS, HB, ACC, XS, XR,
    ssem, rsem, bssem, brsem, lsem,
):
    dp = lax.axis_index("dp")
    sq = lax.axis_index("seq")
    zh, x = lax.div(dp, 4), lax.rem(dp, 4)
    zl, y, c = lax.div(sq, 8), lax.rem(lax.div(sq, 2), 4), lax.rem(sq, 2)

    def dev(zh_=zh, x_=x, zl_=zl, y_=y, c_=c):
        return (zh_ * 4 + x_, zl_ * 8 + y_ * 2 + c_)

    def rot(v, k):
        return lax.rem(v + (k % 4), 4)

    xr, xl, xo = rot(x, 1), rot(x, -1), rot(x, 2)
    yr, yl, yo = rot(y, 1), rot(y, -1), rot(y, 2)
    zr, zf, zo = rot(zh, 1), rot(zh, -1), rot(zh, 2)
    x_right, x_left = dev(x_=xr), dev(x_=xl)
    y_right, y_left = dev(y_=yr), dev(y_=yl)
    z_right, z_left = dev(zh_=zr), dev(zh_=zf)
    nz = 1 - zl
    pair = dev(zl_=nz)
    sibling = dev(c_=1 - c)
    a_to = dev(x_=2 * lax.rem(y, 2) + c, zl_=1 - lax.div(y, 2), y_=x, c_=zl)
    a_from = dev(x_=y, zl_=c, y_=2 * nz + lax.div(x, 2), c_=lax.rem(x, 2))

    wo_row = 2 * lax.div(sq, 2) + 1 - lax.rem(dp, 2)
    wo_to = (wo_row, 2 * lax.div(dp, 2) + c)
    wo_from = (
        2 * lax.div(sq, 2) + 1 - lax.rem(dp, 2), 2 * lax.div(dp, 2) + c
    )

    barrier = pltpu.get_barrier_semaphore()
    greet = [x_right, x_left, y_right, y_left, pair, a_to, a_from, wo_to, wo_from]
    for k in range(1, 8):
        peer = lax.rem(zh * 2 + c + k, 8)
        greet.append(dev(zh_=lax.div(peer, 2), c_=lax.rem(peer, 2)))
    for d in greet:
        pl.semaphore_signal(barrier, inc=1, device_id=d, device_id_type=pl.DeviceIdType.MESH)

    def rows_of(xx):
        return pl.ds(pl.multiple_of(xx * F, 64), F)

    def half_rows(xx, h):
        return pl.ds(pl.multiple_of(xx * F + h * (F // 2), 32), F // 2)

    WB[c, 0, rows_of(x), :] = wk_ref[...]
    WB[c, 1, rows_of(x), :] = wq_ref[...]
    WB[c, 2, rows_of(x), :] = wv_ref[...]
    GB[c, 0] = jnp.broadcast_to(gq_ref[...], (8, 2 * HD))
    GB[c, 1] = jnp.broadcast_to(gk_ref[...], (8, 2 * HD))

    pl.semaphore_wait(barrier, len(greet))

    sent = []

    def send(src, dst, device):
        k = len(sent)
        copy = pltpu.make_async_remote_copy(
            src_ref=src, dst_ref=dst, send_sem=ssem.at[k], recv_sem=rsem.at[k],
            device_id=device, device_id_type=pl.DeviceIdType.MESH,
        )
        copy.start()
        sent.append(copy)
        return copy

    def same(ref, device):
        return send(ref, ref, device)

    def wait(copies):
        for copy in copies:
            copy.wait_recv()

    def w_piece(w, xx):
        return WB.at[c, w, rows_of(xx), :]

    def w_half(w, xx, h):
        return WB.at[c, w, half_rows(xx, h), :]

    w_near, w_far, w_sib = {}, {}, {0: [], 1: [], 2: []}

    def w_start(w):
        w_near[w] = (same(w_piece(w, x), x_right), same(w_piece(w, x), x_left))
        w_sib[w].append(same(w_piece(w, x), sibling))

    def w_relay(w):
        right, left = w_near[w]
        right.wait_recv()
        a = same(w_half(w, xl, 0), x_right)
        w_sib[w].append(same(w_piece(w, xl), sibling))
        left.wait_recv()
        b = same(w_half(w, xr, 1), x_left)
        w_sib[w].append(same(w_piece(w, xr), sibling))
        w_far[w] = (a, b)

    def w_last(w):
        for h in range(2):
            w_far[w][h].wait_recv()
            w_sib[w].append(same(w_half(w, xo, h), sibling))

    def cols_of(g):
        return pl.ds(g * TB, TB)

    def a_piece(z, yy, g):
        return AB.at[z, rows_of(yy), cols_of(g)]

    def a_half(z, yy, h, g):
        return AB.at[z, half_rows(yy, h), cols_of(g)]

    a_perm = [
        send(ref, AB.at[lax.div(y, 2), rows_of(x), cols_of(g)], a_to)
        for g, ref in enumerate((in_ref, tin_ref))
    ]
    wo_perm = send(wo_ref, WOB.at[wo_row], wo_to)

    a_own, a_pair = [], []
    for g in range(2):
        a_perm[g].wait_recv()
        own = a_piece(nz, y, g)
        a_own.append((same(own, y_right), same(own, y_left)))
        a_pair.append(same(own, pair))
        if g == 0:
            w_start(0)
            w_sib[0].append(same(GB.at[c], sibling))

    def wo_block(zz, xx):
        return zz * 4 + xx

    def wo_half(b, h):
        return WOB.at[b, pl.ds(h * (F // 2), F // 2), :]

    w_relay(0)
    a_own_opp = []
    for g, (right, left) in enumerate(a_own):
        right.wait_recv()
        a_own_opp.append(same(a_half(nz, yl, 0, g), y_right))
        left.wait_recv()
        a_own_opp.append(same(a_half(nz, yr, 1, g), y_left))

    wait(a_pair)
    two = AB.at[zl, rows_of(y), :]
    a_two_r, a_two_l = same(two, y_right), same(two, y_left)

    w_start(2)
    wo_perm.wait_recv()
    wo_zr = same(WOB.at[wo_block(zh, x)], z_right)
    wo_zl = same(WOB.at[wo_block(zh, x)], z_left)
    w_last(0)

    def wo_relay_z():
        wo_zr.wait_recv()
        a = same(wo_half(wo_block(zf, x), 0), z_right)
        wo_zl.wait_recv()
        return [a, same(wo_half(wo_block(zr, x), 1), z_left)]

    wo_x = []

    def wo_send_x(zz):
        b = WOB.at[wo_block(zz, x)]
        wo_x.append((zz, same(b, x_right), same(b, x_left)))

    block_at = (nz, zl)

    def turn(t):
        @pl.loop(0, 5)
        def _(i):
            cut = pl.ds(pl.multiple_of(i * 256, 256), 256)
            piece = AB[block_at[t], cut, :].T
            for h in range(2):
                for s in range(2):
                    at = h * TB + s * HALF
                    AN[t, h, s, :, cut] = piece[at:at + HALF, :]

    def tile(kind, k):
        d = rot(zh, k)
        cw = lax.div(d, 2)
        cols = pl.ds(pl.multiple_of(lax.rem(d, 2) * HD, HD), HD)
        queries = kind // 2 == 1
        PART[...] = jnp.zeros((2 * TB, HD), F32)

        @pl.loop(0, 5)
        def _(i):
            deep = pl.ds(pl.multiple_of(i * 256, 256), 256)
            tokens = AN[:, :, kind % 2, :, deep] if queries else AN[kind % 2, :, :, :, deep]
            PART[...] += jnp.dot(
                tokens.reshape(2 * TB, 256), WB[cw, kind // 2, deep, cols],
                preferred_element_type=F32,
            )

        part = PART[...].reshape(2, 2, HALF, HD)
        return [(part[:, h] if queries else part[h]).reshape(TB, HD) for h in range(2)]

    relay, direct, summed = {}, {}, {}

    def rs_send(kind, slot, h, part, to):
        SB[kind, slot, h] = part.astype(BF16)
        return send(SB.at[kind, slot, h], RB.at[kind, slot, h], to)

    def rs_opposite(kind):
        part = tile(kind, 2)
        for h in range(2):
            relay[kind, h] = rs_send(kind, 0, h, part[h], z_right if h == 0 else z_left)

    def rs_direct(kind):
        for slot, k, h, to in ((1, 1, 1, z_right), (2, 3, 0, z_left)):
            part = tile(kind, k)
            direct[kind, slot] = rs_send(kind, slot, h, part[h], to)
            HOLD[kind, 1 - h] = part[1 - h]

    def rs_summed(kind):
        for slot, h, to in ((1, 0, z_right), (2, 1, z_left)):
            relay[kind, h].wait_recv()
            part = HOLD[kind, h] + RB[kind, 0, h].astype(F32)
            summed[kind, slot] = rs_send(kind, slot, h, part, to)

    def rs_own(kind):
        part = tile(kind, 0)
        for h in range(2):
            OWN[kind, h] = part[h]

    def rs_result(kind):
        for slot in (1, 2):
            direct[kind, slot].wait_recv()
            summed[kind, slot].wait_recv()
        return [
            OWN[kind, h] + RB[kind, 1, h].astype(F32) + RB[kind, 2, h].astype(F32)
            for h in range(2)
        ]

    cw = lax.div(zh, 2)
    head_cols = pl.ds(pl.multiple_of(lax.rem(zh, 2) * HD, HD), HD)

    def norm(raw, tan, gain):
        ms = jnp.mean(raw * raw, axis=-1, keepdims=True)
        inv = lax.rsqrt(ms + 1e-06)
        inner = jnp.mean(raw * tan, axis=-1, keepdims=True)
        normed = gain * raw * inv
        normed_tan = gain * inv * (tan - raw * inner * inv * inv)
        return normed.astype(BF16), normed_tan.astype(BF16)

    def slot_of(xx, cc):
        return xx * 2 + cc

    g_near, g_far = {}, {}
    g_sib = {(b, t, j): [] for b in range(2) for t in range(2) for j in range(4)}

    def g_block(b, t, xx, rows=0, count=TB):
        return (KB, VB)[b].at[slot_of(xx, c), pl.ds(t * TB + rows, count), :]

    def g_start(b, t):
        block = g_block(b, t, x)
        g_near[b, t] = (same(block, x_right), same(block, x_left))
        g_sib[b, t, 0].append(same(block, sibling))

    def g_relay(b, t):
        right, left = g_near[b, t]
        right.wait_recv()
        first = same(g_block(b, t, xl, 0, HALF), x_right)
        g_sib[b, t, 1].append(same(g_block(b, t, xl), sibling))
        left.wait_recv()
        second = same(g_block(b, t, xr, HALF, HALF), x_left)
        g_sib[b, t, 2].append(same(g_block(b, t, xr), sibling))
        g_far[b, t] = (first, second)

    def g_last(b, t):
        for h in range(2):
            g_far[b, t][h].wait_recv()
            g_sib[b, t, 3].append(same(g_block(b, t, xo, h * HALF, HALF), sibling))

    def keys_out(t):
        key, key_tan = norm(*rs_result(t), GB[cw, 1, 0:1, head_cols])
        rows = slice(t * TB, (t + 1) * TB)
        KB[slot_of(x, c), rows, 0:HD] = key
        KB[slot_of(x, c), rows, HD:] = key_tan
        g_start(0, t)

    def values_out(t):
        raw, tan = rs_result(4 + t)
        rows = slice(t * TB, (t + 1) * TB)
        VB[slot_of(x, c), rows, 0:HD] = raw.astype(BF16)
        VB[slot_of(x, c), rows, HD:] = tan.astype(BF16)
        g_start(1, t)

    wo_xopp = []

    def wo_relay_x(n):
        zz, right, left = wo_x[n]
        right.wait_recv()
        wo_xopp.append(same(wo_half(wo_block(zz, xl), 0), x_right))
        left.wait_recv()
        wo_xopp.append(same(wo_half(wo_block(zz, xr), 1), x_left))

    to_exp2 = HD ** -0.5 * 1.4426950408889634
    ln2 = 0.6931471805599453
    ROWS = 32

    def queries(s):
        gain = GB[cw, 0, 0:1, head_cols] * to_exp2
        query, query_tan = norm(*rs_result(2 + s), gain)
        QB[s, :, 0:HD] = query_tan
        QB[s, :, HD:] = query

    def arrived(b):
        for t in range(2):
            for j in range(4):
                wait(g_sib[b, t, j])

    def scores(s):
        MX[...] = jnp.full((TB, 128), -jnp.inf, F32)

        @pl.loop(0, 8)
        def _(j):
            keys = KB[j]
            cut = pl.ds(pl.multiple_of(j * 512, 512), 512)
            part = lax.dot_general(
                QB[s, :, HD:], keys[:, :HD], (((1,), (1,)), ((), ())), preferred_element_type=F32
            )
            S[:, cut] = part
            top = jnp.maximum(
                jnp.maximum(part[:, 0:128], part[:, 128:256]),
                jnp.maximum(part[:, 256:384], part[:, 384:512]),
            )
            MX[...] = jnp.maximum(MX[...], top)
            ST[:, cut] = lax.dot_general(
                QB[s], keys, (((1,), (1,)), ((), ())), preferred_element_type=F32
            )

    def softmax(s):
        @pl.loop(0, TB // ROWS)
        def _(i):
            at = pl.multiple_of(i * ROWS, ROWS)
            rows = pl.ds(at, ROWS)
            to = pl.ds(s * TB + at, ROWS)
            shift = jnp.max(MX[rows, :], axis=-1, keepdims=True)
            total = jnp.zeros((ROWS, 128), F32)
            inner = jnp.zeros((ROWS, 128), F32)
            for j in range(16):
                cut = slice(j * 256, (j + 1) * 256)
                e = jnp.exp2(S[rows, cut] - shift)
                EB[to, cut] = e.astype(BF16)
                es = e * ST[rows, cut]
                total += e[:, :128] + e[:, 128:]
                inner += es[:, :128] + es[:, 128:]
            total = jnp.sum(total, axis=-1, keepdims=True)
            mean = jnp.sum(inner, axis=-1, keepdims=True) / total
            LI[to, :] = jnp.broadcast_to(1.0 / total, (ROWS, HD))
            for j in range(16):
                cut = slice(j * 256, (j + 1) * 256)
                UB[to, cut] = (EB[to, cut].astype(F32) * (ST[rows, cut] - mean)).astype(BF16)

    def products(s):
        rows = slice(s * TB, (s + 1) * TB)
        AO[rows, :] = jnp.zeros((TB, 2 * HD), F32)
        AT[rows, :] = jnp.zeros((TB, HD), F32)

        @pl.loop(0, 8)
        def _(j):
            values = VB[j]
            cut = pl.ds(pl.multiple_of(j * 512, 512), 512)
            AO[rows, :] += jnp.dot(EB[rows, cut], values, preferred_element_type=F32)
            AT[rows, :] += jnp.dot(UB[rows, cut], values[:, :HD], preferred_element_type=F32)

    my_pair = zl * 8 + y * 2
    head_at = lax.rem(zh, 2)
    back = []

    def heads_back(s):
        rows = slice(s * TB, (s + 1) * TB)
        inv = LI[rows, :]
        primal = (AO[rows, :HD] * inv).astype(BF16)
        tangent = ((AO[rows, HD:] + AT[rows, :] * ln2) * inv).astype(BF16)
        target = HB.at[my_pair + cw, s, :, head_cols]
        for t in range(2):
            HS[s, t, 0:HALF, :] = primal[t * HALF:(t + 1) * HALF, :]
            HS[s, t, HALF:, :] = tangent[t * HALF:(t + 1) * HALF, :]
            zeta = 2 * c + block_at[t]
            copy = pltpu.make_async_remote_copy(
                src_ref=HS.at[s, t], dst_ref=target, send_sem=bssem.at[2 * s + t],
                recv_sem=brsem.at[2 * s + head_at],
                device_id=dev(zh_=zeta, c_=cw), device_id_type=pl.DeviceIdType.MESH,
            )
            stay = pltpu.make_async_copy(HS.at[s, t], target, lsem.at[2 * s + t])
            here = zeta == zh

            @pl.when(here)
            def _(stay=stay):
                stay.start()
                stay.wait()

            @pl.when(jnp.logical_not(here))
            def _(copy=copy):
                copy.start()

            back.append((copy, here))

    def hp(zz, yy):
        return zz * 8 + yy * 2 + c

    def h_part(p, s):
        return HB.at[p, s]

    def h_half(p, s, h):
        return HB.at[p, s, pl.ds(h * HALF, HALF), :]

    h_own, h_two, h_opp, swapped = {}, {}, {}, {}

    def heads_start(s):
        for h in range(2):
            came = pltpu.make_async_remote_copy(
                src_ref=HS.at[s, h], dst_ref=HB.at[sq, s, :, pl.ds(h * HD, HD)],
                send_sem=bssem.at[2 * s + h], recv_sem=brsem.at[2 * s + h],
                device_id=sibling, device_id_type=pl.DeviceIdType.MESH,
            )

            @pl.when(2 * c + h != zh)
            def _(came=came):
                came.wait_recv()

        mine = h_part(sq, s)
        h_own[s] = (same(mine, y_right), same(mine, y_left), same(mine, pair))

    def heads_pair(s):
        h_own[s][2].wait_recv()
        p = hp(nz, y)
        h_two[s] = (same(h_part(p, s), y_right), same(h_part(p, s), y_left))

    def heads_relay(s, zz, right, left):
        right.wait_recv()
        p = hp(zz, yl)
        first = same(h_half(p, s, 0), y_right)
        left.wait_recv()
        p = hp(zz, yr)
        second = same(h_half(p, s, 1), y_left)
        h_opp.setdefault(s, []).append((zz, first, second))

    def heads_relay_own(s):
        heads_relay(s, zl, *h_own[s][:2])

    def heads_relay_two(s):
        heads_relay(s, nz, *h_two[s])

    def multiply(s, zz, near, first=False):
        total = None if first else ACC[s]
        for yy in (y, yl, yr) if near else (yo,):
            p = hp(zz, yy)
            part = lax.dot_general(
                WOB[pl.ds(p - c, 2)].reshape(2 * F, 2 * HD), HB[p, s], (((1,), (1,)), ((), ())),
                preferred_element_type=F32,
            )
            total = part if total is None else total + part
        ACC[s] = total

    def multiply_far(s):
        for zz, first, second in h_opp[s]:
            first.wait_recv()
            second.wait_recv()
            multiply(s, zz, False)
        XS[s] = ACC[s, pl.ds(pl.multiple_of(c * F, 64), F), :].astype(BF16)
        swapped[s] = send(XS.at[s], XR.at[s], sibling)

    def finish(s):
        swapped[s].wait_recv()
        mine = ACC[s, pl.ds(pl.multiple_of((1 - c) * F, 64), F), :] + XR[s].astype(F32)
        cut = slice(s * HALF, (s + 1) * HALF)
        out_ref[0:F, cut] = mine[:, 0:HALF].astype(BF16)
        out_ref[F:, cut] = mine[:, HALF:].astype(BF16)

    wait(a_own_opp)
    turn(0)
    wait(w_sib[0])
    rs_opposite(0)
    rs_direct(0)
    wo_zopp = wo_relay_z()
    a_two_r.wait_recv()
    a_two_opp = [same(AB.at[zl, half_rows(yl, 0), :], y_right)]
    a_two_l.wait_recv()
    a_two_opp.append(same(AB.at[zl, half_rows(yr, 1), :], y_left))
    w_relay(2)
    w_start(1)
    rs_summed(0)
    rs_own(0)
    wait(a_two_opp)
    turn(1)
    rs_opposite(1)
    rs_direct(1)
    w_last(2)
    w_relay(1)
    for zz in (zh, zf, zr):
        wo_send_x(zz)
    wait(w_sib[2])
    rs_opposite(4)
    rs_summed(1)
    rs_direct(4)
    keys_out(0)
    rs_own(1)
    rs_opposite(5)
    w_last(1)
    rs_summed(4)
    rs_direct(5)
    keys_out(1)
    wait(wo_zopp)
    wo_send_x(zo)
    wait(w_sib[1])
    rs_opposite(2)
    g_relay(0, 0)
    rs_own(4)
    rs_summed(5)
    rs_direct(2)
    g_relay(0, 1)
    values_out(0)
    rs_own(5)
    rs_opposite(3)
    rs_own(2)
    rs_own(3)
    for n in range(4):
        wo_relay_x(n)
    g_last(0, 0)
    g_last(0, 1)
    rs_summed(2)
    rs_direct(3)
    values_out(1)
    g_relay(1, 0)
    rs_summed(3)
    g_last(1, 0)
    g_relay(1, 1)
    queries(0)
    arrived(0)
    scores(0)
    g_last(1, 1)
    softmax(0)
    arrived(1)
    products(0)
    heads_back(0)
    queries(1)
    scores(1)
    wait(wo_xopp)
    heads_start(0)
    softmax(1)
    heads_pair(0)
    heads_relay_own(0)
    products(1)
    heads_back(1)
    multiply(0, zl, True, first=True)
    heads_relay_two(0)
    multiply(0, nz, True)
    heads_start(1)
    heads_pair(1)
    multiply_far(0)
    heads_relay_own(1)
    multiply(1, zl, True, first=True)
    heads_relay_two(1)
    multiply(1, nz, True)
    finish(0)
    multiply_far(1)
    finish(1)

    for copy in sent:
        copy.wait_send()
    for copy, here in back:
        @pl.when(jnp.logical_not(here))
        def _(copy=copy):
            copy.wait_send()


def shards(
    inputs, tangents, query_weight, key_weight, value_weight, query_gain, key_gain, out_weight
):
    vmem = pl.BlockSpec(memory_space=pltpu.VMEM)
    v = pltpu.VMEM
    both = pl.pallas_call(
        kernel,
        out_shape=jax.ShapeDtypeStruct((2 * F, TB), BF16),
        in_specs=[vmem] * 8,
        out_specs=vmem,
        scratch_shapes=[
            v((2, 3, 4 * F, 256), BF16),
            v((2, 2, 8, 256), F32),
            v((2, 4 * F, 512), BF16),
            v((2, 2, 2, HALF, 4 * F), BF16),
            v((16, F, 256), BF16),
            v((2 * TB, HD), F32),
            v((6, 3, 2, TB, HD), BF16),
            v((6, 3, 2, TB, HD), BF16),
            v((6, 2, TB, HD), F32),
            v((6, 2, TB, HD), F32),
            v((8, 512, 256), BF16),
            v((8, 512, 256), BF16),
            v((2, TB, 256), BF16),
            v((TB, TOKENS), F32),
            v((TB, TOKENS), F32),
            v((TB, 128), F32),
            v((2 * TB, HD), F32),
            v((2 * TB, TOKENS), BF16),
            v((2 * TB, TOKENS), BF16),
            v((2 * TB, 2 * HD), F32),
            v((2 * TB, HD), F32),
            v((2, 2, TB, HD), BF16),
            v((16, 2, TB, 256), BF16),
            v((2, 2 * F, TB), F32),
            v((2, F, TB), BF16),
            v((2, F, TB), BF16),
            pltpu.SemaphoreType.DMA((N_SEMS,)),
            pltpu.SemaphoreType.DMA((N_SEMS,)),
            pltpu.SemaphoreType.DMA((4,)),
            pltpu.SemaphoreType.DMA((4,)),
            pltpu.SemaphoreType.DMA((4,)),
        ],
        compiler_params=pltpu.CompilerParams(
            collective_id=0, has_side_effects=True, vmem_limit_bytes=60 * 2**20
        ),
    )(
        inputs.T, tangents.T, query_weight, key_weight, value_weight,
        query_gain.reshape(1, 2 * HD), key_gain.reshape(1, 2 * HD), out_weight.T,
    )
    return both[:F].T, both[F:].T


def solution(mesh):
    in_specs = (
        P("seq", "dp"),
        P("seq", "dp"),
        P("dp", "seq"),
        P("dp", "seq"),
        P("dp", "seq"),
        P("seq"),
        P("seq"),
        P("seq", "dp"),
    )
    out_specs = (P("dp", "seq"), P("dp", "seq"))
    return jax.shard_map(shards, mesh=mesh, in_specs=in_specs, out_specs=out_specs, check_vma=False)
```

time: 544 us -> 154 us (0.28)
  waiting for transfers between devices: 449 us -> 0 us
  Pallas kernels: 0 us -> 151 us
  matrix products: 54.6 us -> 0 us
  other arithmetic: 14 us -> 0 us
  between operations: 14.3 us -> 0.64 us
  local copies, waits for them, and re-layouts: 8.39 us -> 1.74 us
    reduce_scatter x2 -> x0, waiting for transfers between devices: 226 us -> none  [the longest x1 160 us: shards(): lax.psum_scatter(jnp.concatenate([jnp.dot(whole, all_weights, preferred_e...]
    all_gather x4 -> x0, waiting for transfers between devices: 221 us -> none  [the longest x1 101 us: shards(): gathered = lax.all_gather(stacked, 'dp', axis=1, tiled=True)]
    pallas_call x0 -> x1, Pallas kernels: none -> 151 us  [shards(): pl.pallas_call(kernel, out_shape=jax.ShapeDtypeStruct((2 * F, TB), BF16),...]
    dot_general x8 -> x0, matrix products: 47.2 us -> none  [the longest x1 8.58 us: attend(): jnp.einsum('hqk,khd->qhd', probs_tan_b, values, preferred_element_type=jn...]
    concatenate x1 -> x0, other arithmetic: 11.4 us -> none  [shards(): jnp.concatenate([jnp.dot(whole, all_weights, preferred_element_type=jnp.f...]
    sub x1 -> x0, matrix products: 7.37 us -> none  [attend(): expo = jnp.exp(scores - top)]
  transfers between devices with their start and end apart: 6 -> 0, of which waited for: 6 -> 0; matrix products, arithmetic and copies ran while one was open for 9% -> 0% of each run, Pallas kernels for 0% -> 0%
where the time goes in v1:
time: 154 us; the launch traced here: 153 us
  Pallas kernels  151 us (98%)
  local copies, waits for them, and re-layouts  1.74 us (1%)
    pallas_call x1, Pallas kernels, shards(): pl.pallas_call(kernel, out_shape=jax.ShapeDtypeStruct((2 * F, TB), BF16),...  151 us

profile of v1, /device:TPU:1, one launch (start us, length us, event | category | flops | bytes accessed | tf_op | source)
XLA Modules:
  0.0 153.2 jit_solution(6149310608432473518)
XLA Ops:
  0.6 150.9 %shard_map.95 = bf16[640,256]{1,0:T(8,128)(2,1)} custom-call(bf16[320,256]{1,0:T(8,128)(2,1)} %bitcast.9, bf16[320,256]{1,0:T(8,128)(2,1)} %bitcast.10, bf16[320,256]{1,0:T(8,128)(2,1)} %wq_ref.1, bf16[320,256]{1,0:T(8,128)(2,1)} %wk_ref.1, bf16[320,256]{1,0:T(8,128)(2,1)} %wv_ref.1, f32[1,256]{1,0:T(1,128)} %bitcast.12, f32[1,256]{1,0:T(1,128)} %bitcast.13, ...), custom_call_target="tpu_custom_call" | custom-call | tf_op jit(solution)/shard_map/pallas_call | solution.py:590
  151.5 1.7 %slice_bitcast_fusion = (bf16[256,320]{0,1:T(8,128)(2,1)}, bf16[256,320]{0,1:T(8,128)(2,1)}) fusion(bf16[640,256]{1,0:T(8,128)(2,1)} %shard_map.95), kind=kLoop, calls=%fused_computation | loop fusion | bytes 655360 | tf_op jit(solution)/shard_map/transpose | solution.py:635

commit v2 on v1

--- a/solution.py
+++ b/solution.py
@@ -29,12 +29,12 @@
     def dev(zh_=zh, x_=x, zl_=zl, y_=y, c_=c):
         return (zh_ * 4 + x_, zl_ * 8 + y_ * 2 + c_)
 
-    def rot(v, k):
-        return lax.rem(v + (k % 4), 4)
-
-    xr, xl, xo = rot(x, 1), rot(x, -1), rot(x, 2)
-    yr, yl, yo = rot(y, 1), rot(y, -1), rot(y, 2)
-    zr, zf, zo = rot(zh, 1), rot(zh, -1), rot(zh, 2)
+    def ring(v):
+        return lax.rem(v + 1 + 2 * c, 4), lax.rem(v + 3 - 2 * c, 4), lax.rem(v + 2, 4)
+
+    xr, xl, xo = ring(x)
+    yr, yl, yo = ring(y)
+    zr, zf, zo = ring(zh)
     x_right, x_left = dev(x_=xr), dev(x_=xl)
     y_right, y_left = dev(y_=yr), dev(y_=yl)
     z_right, z_left = dev(zh_=zr), dev(zh_=zf)
@@ -192,7 +192,7 @@
                     AN[t, h, s, :, cut] = piece[at:at + HALF, :]
 
     def tile(kind, k):
-        d = rot(zh, k)
+        d = (zh, zr, zo, zf)[k]
         cw = lax.div(d, 2)
         cols = pl.ds(pl.multiple_of(lax.rem(d, 2) * HD, HD), HD)
         queries = kind // 2 == 1

time: 154 us -> 154 us (level)
  no operation moved by 1% of the time
where the time goes in v2:
time: 154 us
  Pallas kernels  151 us (98%)
  local copies, waits for them, and re-layouts  1.74 us (1%)
    pallas_call x1, Pallas kernels, shards(): pl.pallas_call(kernel, out_shape=jax.ShapeDtypeStruct((2 * F, TB), BF16),...  151 us

profile of v2, /device:TPU:1, one launch (start us, length us, event | category | flops | bytes accessed | tf_op | source)
XLA Modules:
  0.0 153.7 jit_solution(7085480251173373132)
XLA Ops:
  0.6 151.3 %shard_map.95 = bf16[640,256]{1,0:T(8,128)(2,1)} custom-call(bf16[320,256]{1,0:T(8,128)(2,1)} %bitcast.9, bf16[320,256]{1,0:T(8,128)(2,1)} %bitcast.10, bf16[320,256]{1,0:T(8,128)(2,1)} %wq_ref.1, bf16[320,256]{1,0:T(8,128)(2,1)} %wk_ref.1, bf16[320,256]{1,0:T(8,128)(2,1)} %wv_ref.1, f32[1,256]{1,0:T(1,128)} %bitcast.12, f32[1,256]{1,0:T(1,128)} %bitcast.13, ...), custom_call_target="tpu_custom_call" | custom-call | tf_op jit(solution)/shard_map/pallas_call | solution.py:590
  151.9 1.7 %slice_bitcast_fusion = (bf16[256,320]{0,1:T(8,128)(2,1)}, bf16[256,320]{0,1:T(8,128)(2,1)}) fusion(bf16[640,256]{1,0:T(8,128)(2,1)} %shard_map.95), kind=kLoop, calls=%fused_computation | loop fusion | bytes 655360 | tf_op jit(solution)/shard_map/transpose | solution.py:635

commit v3 on v2

--- a/solution.py
+++ b/solution.py
@@ -131,7 +131,6 @@
         send(ref, AB.at[lax.div(y, 2), rows_of(x), cols_of(g)], a_to)
         for g, ref in enumerate((in_ref, tin_ref))
     ]
-    wo_perm = send(wo_ref, WOB.at[wo_row], wo_to)
 
     a_own, a_pair = [], []
     for g in range(2):
@@ -140,6 +139,7 @@
         a_own.append((same(own, y_right), same(own, y_left)))
         a_pair.append(same(own, pair))
         if g == 0:
+            wo_perm = send(wo_ref, WOB.at[wo_row], wo_to)
             w_start(0)
             w_sib[0].append(same(GB.at[c], sibling))
 
@@ -161,17 +161,20 @@
     two = AB.at[zl, rows_of(y), :]
     a_two_r, a_two_l = same(two, y_right), same(two, y_left)
 
+    def wo_start_z():
+        block = WOB.at[wo_block(zh, x)]
+        return same(block, z_right), same(block, z_left)
+
+    def wo_relay_z():
+        return [
+            same(wo_half(wo_block(zf, x), 0), z_right),
+            same(wo_half(wo_block(zr, x), 1), z_left),
+        ]
+
     w_start(2)
     wo_perm.wait_recv()
-    wo_zr = same(WOB.at[wo_block(zh, x)], z_right)
-    wo_zl = same(WOB.at[wo_block(zh, x)], z_left)
+    wo_z = wo_start_z()
     w_last(0)
-
-    def wo_relay_z():
-        wo_zr.wait_recv()
-        a = same(wo_half(wo_block(zf, x), 0), z_right)
-        wo_zl.wait_recv()
-        return [a, same(wo_half(wo_block(zr, x), 1), z_left)]
 
     wo_x = []
 
@@ -389,91 +392,99 @@
         inv = LI[rows, :]
         primal = (AO[rows, :HD] * inv).astype(BF16)
         tangent = ((AO[rows, HD:] + AT[rows, :] * ln2) * inv).astype(BF16)
-        target = HB.at[my_pair + cw, s, :, head_cols]
         for t in range(2):
             HS[s, t, 0:HALF, :] = primal[t * HALF:(t + 1) * HALF, :]
             HS[s, t, HALF:, :] = tangent[t * HALF:(t + 1) * HALF, :]
-            zeta = 2 * c + block_at[t]
-            copy = pltpu.make_async_remote_copy(
-                src_ref=HS.at[s, t], dst_ref=target, send_sem=bssem.at[2 * s + t],
-                recv_sem=brsem.at[2 * s + head_at],
-                device_id=dev(zh_=zeta, c_=cw), device_id_type=pl.DeviceIdType.MESH,
-            )
-            stay = pltpu.make_async_copy(HS.at[s, t], target, lsem.at[2 * s + t])
-            here = zeta == zh
-
-            @pl.when(here)
-            def _(stay=stay):
-                stay.start()
-                stay.wait()
-
-            @pl.when(jnp.logical_not(here))
-            def _(copy=copy):
-                copy.start()
-
-            back.append((copy, here))
+        for g in range(2):
+            q = 2 * s + g
+            target = HB.at[my_pair + cw, q, :, head_cols]
+            for t in range(2):
+                zeta = 2 * c + block_at[t]
+                source = HS.at[s, t, pl.ds(g * HALF, HALF), :]
+                copy = pltpu.make_async_remote_copy(
+                    src_ref=source, dst_ref=target, send_sem=bssem.at[2 * q + t],
+                    recv_sem=brsem.at[2 * q + head_at],
+                    device_id=dev(zh_=zeta, c_=cw), device_id_type=pl.DeviceIdType.MESH,
+                )
+                stay = pltpu.make_async_copy(source, target, lsem.at[2 * q + t])
+                here = zeta == zh
+
+                @pl.when(here)
+                def _(stay=stay):
+                    stay.start()
+                    stay.wait()
+
+                @pl.when(jnp.logical_not(here))
+                def _(copy=copy):
+                    copy.start()
+
+                back.append((copy, here))
 
     def hp(zz, yy):
         return zz * 8 + yy * 2 + c
 
-    def h_part(p, s):
-        return HB.at[p, s]
-
-    def h_half(p, s, h):
-        return HB.at[p, s, pl.ds(h * HALF, HALF), :]
+    def h_part(p, q):
+        return HB.at[p, q]
+
+    def h_half(p, q, h):
+        return HB.at[p, q, pl.ds(h * (HALF // 2), HALF // 2), :]
 
     h_own, h_two, h_opp, swapped = {}, {}, {}, {}
 
     def heads_start(s):
-        for h in range(2):
-            came = pltpu.make_async_remote_copy(
-                src_ref=HS.at[s, h], dst_ref=HB.at[sq, s, :, pl.ds(h * HD, HD)],
-                send_sem=bssem.at[2 * s + h], recv_sem=brsem.at[2 * s + h],
-                device_id=sibling, device_id_type=pl.DeviceIdType.MESH,
-            )
-
-            @pl.when(2 * c + h != zh)
-            def _(came=came):
-                came.wait_recv()
-
-        mine = h_part(sq, s)
-        h_own[s] = (same(mine, y_right), same(mine, y_left), same(mine, pair))
+        for q in (2 * s, 2 * s + 1):
+            for h in range(2):
+                came = pltpu.make_async_remote_copy(
+                    src_ref=HS.at[s, h, pl.ds(0, HALF), :],
+                    dst_ref=HB.at[sq, q, :, pl.ds(h * HD, HD)],
+                    send_sem=bssem.at[2 * q + h], recv_sem=brsem.at[2 * q + h],
+                    device_id=sibling, device_id_type=pl.DeviceIdType.MESH,
+                )
+
+                @pl.when(2 * c + h != zh)
+                def _(came=came):
+                    came.wait_recv()
+
+            mine = h_part(sq, q)
+            across = same(mine, pair)
+            h_own[q] = (same(mine, y_right), same(mine, y_left), across)
 
     def heads_pair(s):
-        h_own[s][2].wait_recv()
-        p = hp(nz, y)
-        h_two[s] = (same(h_part(p, s), y_right), same(h_part(p, s), y_left))
-
-    def heads_relay(s, zz, right, left):
-        right.wait_recv()
-        p = hp(zz, yl)
-        first = same(h_half(p, s, 0), y_right)
-        left.wait_recv()
-        p = hp(zz, yr)
-        second = same(h_half(p, s, 1), y_left)
-        h_opp.setdefault(s, []).append((zz, first, second))
+        for q in (2 * s, 2 * s + 1):
+            h_own[q][2].wait_recv()
+            p = hp(nz, y)
+            h_two[q] = (same(h_part(p, q), y_right), same(h_part(p, q), y_left))
+
+    def heads_relay(s, zz, arrivals):
+        for q in (2 * s, 2 * s + 1):
+            right, left = arrivals[q][:2]
+            right.wait_recv()
+            first = same(h_half(hp(zz, yl), q, 0), y_right)
+            left.wait_recv()
+            second = same(h_half(hp(zz, yr), q, 1), y_left)
+            h_opp.setdefault((s, zz is zl), []).extend([first, second])
 
     def heads_relay_own(s):
-        heads_relay(s, zl, *h_own[s][:2])
+        heads_relay(s, zl, h_own)
 
     def heads_relay_two(s):
-        heads_relay(s, nz, *h_two[s])
+        heads_relay(s, nz, h_two)
 
     def multiply(s, zz, near, first=False):
         total = None if first else ACC[s]
         for yy in (y, yl, yr) if near else (yo,):
             p = hp(zz, yy)
             part = lax.dot_general(
-                WOB[pl.ds(p - c, 2)].reshape(2 * F, 2 * HD), HB[p, s], (((1,), (1,)), ((), ())),
+                WOB[pl.ds(p - c, 2)].reshape(2 * F, 2 * HD),
+                HB[p, 2 * s:2 * s + 2].reshape(TB, 2 * HD), (((1,), (1,)), ((), ())),
                 preferred_element_type=F32,
             )
             total = part if total is None else total + part
         ACC[s] = total
 
     def multiply_far(s):
-        for zz, first, second in h_opp[s]:
-            first.wait_recv()
-            second.wait_recv()
+        for zz in (zl, nz):
+            wait(h_opp[s, zz is zl])
             multiply(s, zz, False)
         XS[s] = ACC[s, pl.ds(pl.multiple_of(c * F, 64), F), :].astype(BF16)
         swapped[s] = send(XS.at[s], XR.at[s], sibling)
@@ -490,23 +501,24 @@
     wait(w_sib[0])
     rs_opposite(0)
     rs_direct(0)
-    wo_zopp = wo_relay_z()
     a_two_r.wait_recv()
     a_two_opp = [same(AB.at[zl, half_rows(yl, 0), :], y_right)]
     a_two_l.wait_recv()
     a_two_opp.append(same(AB.at[zl, half_rows(yr, 1), :], y_left))
     w_relay(2)
     w_start(1)
+    rs_own(0)
     rs_summed(0)
-    rs_own(0)
     wait(a_two_opp)
     turn(1)
     rs_opposite(1)
     rs_direct(1)
     w_last(2)
     w_relay(1)
-    for zz in (zh, zf, zr):
-        wo_send_x(zz)
+    wo_send_x(zh)
+    wait(wo_z)
+    wo_send_x(zf)
+    wo_send_x(zr)
     wait(w_sib[2])
     rs_opposite(4)
     rs_summed(1)
@@ -518,8 +530,6 @@
     rs_summed(4)
     rs_direct(5)
     keys_out(1)
-    wait(wo_zopp)
-    wo_send_x(zo)
     wait(w_sib[1])
     rs_opposite(2)
     g_relay(0, 0)
@@ -532,15 +542,16 @@
     rs_opposite(3)
     rs_own(2)
     rs_own(3)
-    for n in range(4):
-        wo_relay_x(n)
     g_last(0, 0)
     g_last(0, 1)
+    for n in range(3):
+        wo_relay_x(n)
     rs_summed(2)
     rs_direct(3)
     values_out(1)
     g_relay(1, 0)
     rs_summed(3)
+    wo_zopp = wo_relay_z()
     g_last(1, 0)
     g_relay(1, 1)
     queries(0)
@@ -553,25 +564,28 @@
     heads_back(0)
     queries(1)
     scores(1)
-    wait(wo_xopp)
     heads_start(0)
     softmax(1)
+    wait(wo_zopp)
+    wo_send_x(zo)
     heads_pair(0)
     heads_relay_own(0)
     products(1)
     heads_back(1)
+    heads_relay_two(0)
+    heads_start(1)
+    wo_relay_x(3)
+    heads_pair(1)
+    heads_relay_own(1)
+    wait(wo_xopp)
     multiply(0, zl, True, first=True)
-    heads_relay_two(0)
     multiply(0, nz, True)
-    heads_start(1)
-    heads_pair(1)
     multiply_far(0)
-    heads_relay_own(1)
+    heads_relay_two(1)
     multiply(1, zl, True, first=True)
-    heads_relay_two(1)
     multiply(1, nz, True)
+    multiply_far(1)
     finish(0)
-    multiply_far(1)
     finish(1)
 
     for copy in sent:
@@ -615,15 +629,15 @@
             v((2 * TB, 2 * HD), F32),
             v((2 * TB, HD), F32),
             v((2, 2, TB, HD), BF16),
-            v((16, 2, TB, 256), BF16),
+            v((16, 4, HALF, 256), BF16),
             v((2, 2 * F, TB), F32),
             v((2, F, TB), BF16),
             v((2, F, TB), BF16),
             pltpu.SemaphoreType.DMA((N_SEMS,)),
             pltpu.SemaphoreType.DMA((N_SEMS,)),
-            pltpu.SemaphoreType.DMA((4,)),
-            pltpu.SemaphoreType.DMA((4,)),
-            pltpu.SemaphoreType.DMA((4,)),
+            pltpu.SemaphoreType.DMA((8,)),
+            pltpu.SemaphoreType.DMA((8,)),
+            pltpu.SemaphoreType.DMA((8,)),
         ],
         compiler_params=pltpu.CompilerParams(
             collective_id=0, has_side_effects=True, vmem_limit_bytes=60 * 2**20

time: 154 us -> 149 us (0.968)
  Pallas kernels: 151 us -> 146 us
    pallas_call x1, Pallas kernels: 151 us -> 146 us  [shards(): pl.pallas_call(kernel, out_shape=jax.ShapeDtypeStruct((2 * F, TB), BF16),...]
where the time goes in v3:
time: 149 us
  Pallas kernels  146 us (98%)
  local copies, waits for them, and re-layouts  1.74 us (1%)
    pallas_call x1, Pallas kernels, shards(): pl.pallas_call(kernel, out_shape=jax.ShapeDtypeStruct((2 * F, TB), BF16),...  146 us

profile of v3, /device:TPU:1, one launch (start us, length us, event | category | flops | bytes accessed | tf_op | source)
XLA Modules:
  0.0 148.7 jit_solution(6776001162960517709)
XLA Ops:
  0.6 146.4 %shard_map.95 = bf16[640,256]{1,0:T(8,128)(2,1)} custom-call(bf16[320,256]{1,0:T(8,128)(2,1)} %bitcast.9, bf16[320,256]{1,0:T(8,128)(2,1)} %bitcast.10, bf16[320,256]{1,0:T(8,128)(2,1)} %wq_ref.1, bf16[320,256]{1,0:T(8,128)(2,1)} %wk_ref.1, bf16[320,256]{1,0:T(8,128)(2,1)} %wv_ref.1, f32[1,256]{1,0:T(1,128)} %bitcast.12, f32[1,256]{1,0:T(1,128)} %bitcast.13, ...), custom_call_target="tpu_custom_call" | custom-call | tf_op jit(solution)/shard_map/pallas_call | solution.py:604
  147.0 1.7 %slice_bitcast_fusion = (bf16[256,320]{0,1:T(8,128)(2,1)}, bf16[256,320]{0,1:T(8,128)(2,1)}) fusion(bf16[640,256]{1,0:T(8,128)(2,1)} %shard_map.95), kind=kLoop, calls=%fused_computation | loop fusion | bytes 655360 | tf_op jit(solution)/shard_map/transpose | solution.py:649

commit v4 on v3

--- a/solution.py
+++ b/solution.py
@@ -18,7 +18,7 @@
 def kernel(
     in_ref, tin_ref, wq_ref, wk_ref, wv_ref, gq_ref, gk_ref, wo_ref,
     out_ref,
-    WB, GB, AB, AN, WOB, PART, SB, RB, HOLD, OWN, KB, VB, QB, S, ST, MX, LI, EB, UB, AO, AT, HS, HB, ACC, XS, XR,
+    WB, GB, AB, AN, WOB, PART, SB, RB, HOLD, OWN, KB, VB, QB, S, MX, LI, EB, AO, HS, HB, ACC, XS, XR,
     ssem, rsem, bssem, brsem, lsem,
 ):
     dp = lax.axis_index("dp")
@@ -184,15 +184,13 @@
 
     block_at = (nz, zl)
 
-    def turn(t):
+    def turn(t, h):
         @pl.loop(0, 5)
         def _(i):
             cut = pl.ds(pl.multiple_of(i * 256, 256), 256)
-            piece = AB[block_at[t], cut, :].T
-            for h in range(2):
-                for s in range(2):
-                    at = h * TB + s * HALF
-                    AN[t, h, s, :, cut] = piece[at:at + HALF, :]
+            piece = AB[block_at[t], cut, h * TB:(h + 1) * TB].T
+            for s in range(2):
+                AN[t, h, s, :, cut] = piece[s * HALF:(s + 1) * HALF, :]
 
     def tile(kind, k):
         d = (zh, zr, zo, zf)[k]
@@ -320,8 +318,10 @@
     def queries(s):
         gain = GB[cw, 0, 0:1, head_cols] * to_exp2
         query, query_tan = norm(*rs_result(2 + s), gain)
-        QB[s, :, 0:HD] = query_tan
-        QB[s, :, HD:] = query
+        QB[0:TB, 0:HD] = query_tan
+        QB[0:TB, HD:] = query
+        QB[TB:, 0:HD] = query
+        QB[TB:, HD:] = jnp.zeros((TB, HD), BF16)
 
     def arrived(b):
         for t in range(2):
@@ -333,65 +333,57 @@
 
         @pl.loop(0, 8)
         def _(j):
-            keys = KB[j]
             cut = pl.ds(pl.multiple_of(j * 512, 512), 512)
             part = lax.dot_general(
-                QB[s, :, HD:], keys[:, :HD], (((1,), (1,)), ((), ())), preferred_element_type=F32
+                QB[...], KB[j], (((1,), (1,)), ((), ())), preferred_element_type=F32
             )
             S[:, cut] = part
+            part = part[TB:]
             top = jnp.maximum(
                 jnp.maximum(part[:, 0:128], part[:, 128:256]),
                 jnp.maximum(part[:, 256:384], part[:, 384:512]),
             )
             MX[...] = jnp.maximum(MX[...], top)
-            ST[:, cut] = lax.dot_general(
-                QB[s], keys, (((1,), (1,)), ((), ())), preferred_element_type=F32
-            )
 
     def softmax(s):
         @pl.loop(0, TB // ROWS)
         def _(i):
             at = pl.multiple_of(i * ROWS, ROWS)
             rows = pl.ds(at, ROWS)
-            to = pl.ds(s * TB + at, ROWS)
+            raw = pl.ds(TB + at, ROWS)
             shift = jnp.max(MX[rows, :], axis=-1, keepdims=True)
             total = jnp.zeros((ROWS, 128), F32)
             inner = jnp.zeros((ROWS, 128), F32)
             for j in range(16):
                 cut = slice(j * 256, (j + 1) * 256)
-                e = jnp.exp2(S[rows, cut] - shift)
-                EB[to, cut] = e.astype(BF16)
-                es = e * ST[rows, cut]
+                e = jnp.exp2(S[raw, cut] - shift)
+                EB[rows, cut] = e.astype(BF16)
+                es = e * S[rows, cut]
                 total += e[:, :128] + e[:, 128:]
                 inner += es[:, :128] + es[:, 128:]
             total = jnp.sum(total, axis=-1, keepdims=True)
             mean = jnp.sum(inner, axis=-1, keepdims=True) / total
-            LI[to, :] = jnp.broadcast_to(1.0 / total, (ROWS, HD))
+            LI[rows, :] = jnp.broadcast_to(1.0 / total, (ROWS, HD))
             for j in range(16):
                 cut = slice(j * 256, (j + 1) * 256)
-                UB[to, cut] = (EB[to, cut].astype(F32) * (ST[rows, cut] - mean)).astype(BF16)
+                EB[raw, cut] = (EB[rows, cut].astype(F32) * (S[rows, cut] - mean)).astype(BF16)
 
     def products(s):
-        rows = slice(s * TB, (s + 1) * TB)
-        AO[rows, :] = jnp.zeros((TB, 2 * HD), F32)
-        AT[rows, :] = jnp.zeros((TB, HD), F32)
+        AO[...] = jnp.zeros((2 * TB, 2 * HD), F32)
 
         @pl.loop(0, 8)
         def _(j):
-            values = VB[j]
             cut = pl.ds(pl.multiple_of(j * 512, 512), 512)
-            AO[rows, :] += jnp.dot(EB[rows, cut], values, preferred_element_type=F32)
-            AT[rows, :] += jnp.dot(UB[rows, cut], values[:, :HD], preferred_element_type=F32)
+            AO[...] += jnp.dot(EB[:, cut], VB[j], preferred_element_type=F32)
 
     my_pair = zl * 8 + y * 2
     head_at = lax.rem(zh, 2)
     back = []
 
     def heads_back(s):
-        rows = slice(s * TB, (s + 1) * TB)
-        inv = LI[rows, :]
-        primal = (AO[rows, :HD] * inv).astype(BF16)
-        tangent = ((AO[rows, HD:] + AT[rows, :] * ln2) * inv).astype(BF16)
+        inv = LI[...]
+        primal = (AO[0:TB, :HD] * inv).astype(BF16)
+        tangent = ((AO[0:TB, HD:] + AO[TB:, :HD] * ln2) * inv).astype(BF16)
         for t in range(2):
             HS[s, t, 0:HALF, :] = primal[t * HALF:(t + 1) * HALF, :]
             HS[s, t, HALF:, :] = tangent[t * HALF:(t + 1) * HALF, :]
@@ -496,8 +488,9 @@
         out_ref[0:F, cut] = mine[:, 0:HALF].astype(BF16)
         out_ref[F:, cut] = mine[:, HALF:].astype(BF16)
 
-    wait(a_own_opp)
-    turn(0)
+    for h in range(2):
+        wait(a_own_opp[2 * h:2 * h + 2])
+        turn(0, h)
     wait(w_sib[0])
     rs_opposite(0)
     rs_direct(0)
@@ -510,7 +503,8 @@
     rs_own(0)
     rs_summed(0)
     wait(a_two_opp)
-    turn(1)
+    turn(1, 0)
+    turn(1, 1)
     rs_opposite(1)
     rs_direct(1)
     w_last(2)
@@ -619,15 +613,12 @@
             v((6, 2, TB, HD), F32),
             v((8, 512, 256), BF16),
             v((8, 512, 256), BF16),
-            v((2, TB, 256), BF16),
-            v((TB, TOKENS), F32),
-            v((TB, TOKENS), F32),
+            v((2 * TB, 256), BF16),
+            v((2 * TB, TOKENS), F32),
             v((TB, 128), F32),
-            v((2 * TB, HD), F32),
-            v((2 * TB, TOKENS), BF16),
+            v((TB, HD), F32),
             v((2 * TB, TOKENS), BF16),
             v((2 * TB, 2 * HD), F32),
-            v((2 * TB, HD), F32),
             v((2, 2, TB, HD), BF16),
             v((16, 4, HALF, 256), BF16),
             v((2, 2 * F, TB), F32),

time: 149 us -> 150 us (level)
  Pallas kernels: 146 us -> 148 us
where the time goes in v4:
time: 150 us
  Pallas kernels  148 us (99%)
  local copies, waits for them, and re-layouts  1.74 us (1%)
    pallas_call x1, Pallas kernels, shards(): pl.pallas_call(kernel, out_shape=jax.ShapeDtypeStruct((2 * F, TB), BF16),...  148 us

profile of v4, /device:TPU:1, one launch (start us, length us, event | category | flops | bytes accessed | tf_op | source)
XLA Modules:
  0.0 150.1 jit_solution(369062896143862008)
XLA Ops:
  0.6 147.7 %shard_map.95 = bf16[640,256]{1,0:T(8,128)(2,1)} custom-call(bf16[320,256]{1,0:T(8,128)(2,1)} %bitcast.9, bf16[320,256]{1,0:T(8,128)(2,1)} %bitcast.10, bf16[320,256]{1,0:T(8,128)(2,1)} %wq_ref.1, bf16[320,256]{1,0:T(8,128)(2,1)} %wk_ref.1, bf16[320,256]{1,0:T(8,128)(2,1)} %wv_ref.1, f32[1,256]{1,0:T(1,128)} %bitcast.12, f32[1,256]{1,0:T(1,128)} %bitcast.13, ...), custom_call_target="tpu_custom_call" | custom-call | tf_op jit(solution)/shard_map/pallas_call | solution.py:598
  148.4 1.7 %slice_bitcast_fusion = (bf16[256,320]{0,1:T(8,128)(2,1)}, bf16[256,320]{0,1:T(8,128)(2,1)}) fusion(bf16[640,256]{1,0:T(8,128)(2,1)} %shard_map.95), kind=kLoop, calls=%fused_computation | loop fusion | bytes 655360 | tf_op jit(solution)/shard_map/transpose | solution.py:640

commit v5 on v4

--- a/solution.py
+++ b/solution.py
@@ -12,7 +12,7 @@
 HALF = 128
 BF16 = jnp.bfloat16
 F32 = jnp.float32
-N_SEMS = 192
+N_SEMS = 208
 
 
 def kernel(
@@ -121,27 +121,28 @@
     def cols_of(g):
         return pl.ds(g * TB, TB)
 
-    def a_piece(z, yy, g):
-        return AB.at[z, rows_of(yy), cols_of(g)]
-
-    def a_half(z, yy, h, g):
-        return AB.at[z, half_rows(yy, h), cols_of(g)]
-
-    a_perm = [
-        send(ref, AB.at[lax.div(y, 2), rows_of(x), cols_of(g)], a_to)
-        for g, ref in enumerate((in_ref, tin_ref))
-    ]
-
-    a_own, a_pair = [], []
-    for g in range(2):
-        a_perm[g].wait_recv()
-        own = a_piece(nz, y, g)
+    def a_chunk(z, yy, k):
+        return AB.at[z, half_rows(yy, k % 2), cols_of(k // 2)]
+
+    a_perm = []
+    for k in range(4):
+        ref = (in_ref, tin_ref)[k // 2].at[pl.ds((k % 2) * (F // 2), F // 2), :]
+        a_perm.append(
+            send(ref, AB.at[lax.div(y, 2), half_rows(x, k % 2), cols_of(k // 2)], a_to)
+        )
+
+    a_own, a_pair, a_two, a_own_opp, a_two_opp = [], [], [], [], []
+
+    def a_start(k):
+        a_perm[k].wait_recv()
+        own = a_chunk(nz, y, k)
         a_own.append((same(own, y_right), same(own, y_left)))
         a_pair.append(same(own, pair))
-        if g == 0:
-            wo_perm = send(wo_ref, WOB.at[wo_row], wo_to)
-            w_start(0)
-            w_sib[0].append(same(GB.at[c], sibling))
+
+    def a_relay(z, arrivals, k):
+        arrivals[k][k % 2].wait_recv()
+        yy, to = ((yl, y_right), (yr, y_left))[k % 2]
+        return same(a_chunk(z, yy, k), to)
 
     def wo_block(zz, xx):
         return zz * 4 + xx
@@ -149,17 +150,22 @@
     def wo_half(b, h):
         return WOB.at[b, pl.ds(h * (F // 2), F // 2), :]
 
+    a_start(0)
+    a_start(1)
+    wo_perm = send(wo_ref, WOB.at[wo_row], wo_to)
+    w_start(0)
+    w_sib[0].append(same(GB.at[c], sibling))
+    a_start(2)
+    a_own_opp.append(a_relay(nz, a_own, 0))
+    a_start(3)
+    a_own_opp.append(a_relay(nz, a_own, 1))
     w_relay(0)
-    a_own_opp = []
-    for g, (right, left) in enumerate(a_own):
-        right.wait_recv()
-        a_own_opp.append(same(a_half(nz, yl, 0, g), y_right))
-        left.wait_recv()
-        a_own_opp.append(same(a_half(nz, yr, 1, g), y_left))
-
-    wait(a_pair)
-    two = AB.at[zl, rows_of(y), :]
-    a_two_r, a_two_l = same(two, y_right), same(two, y_left)
+    a_own_opp.append(a_relay(nz, a_own, 2))
+    a_own_opp.append(a_relay(nz, a_own, 3))
+    for k in range(4):
+        a_pair[k].wait_recv()
+        two = a_chunk(zl, y, k)
+        a_two.append((same(two, y_right), same(two, y_left)))
 
     def wo_start_z():
         block = WOB.at[wo_block(zh, x)]
@@ -490,21 +496,23 @@
 
     for h in range(2):
         wait(a_own_opp[2 * h:2 * h + 2])
+        for k in (2 * h, 2 * h + 1):
+            a_own[k][1 - k % 2].wait_recv()
         turn(0, h)
     wait(w_sib[0])
     rs_opposite(0)
     rs_direct(0)
-    a_two_r.wait_recv()
-    a_two_opp = [same(AB.at[zl, half_rows(yl, 0), :], y_right)]
-    a_two_l.wait_recv()
-    a_two_opp.append(same(AB.at[zl, half_rows(yr, 1), :], y_left))
+    for k in range(4):
+        a_two_opp.append(a_relay(zl, a_two, k))
     w_relay(2)
     w_start(1)
     rs_own(0)
     rs_summed(0)
-    wait(a_two_opp)
-    turn(1, 0)
-    turn(1, 1)
+    for h in range(2):
+        wait(a_two_opp[2 * h:2 * h + 2])
+        for k in (2 * h, 2 * h + 1):
+            a_two[k][1 - k % 2].wait_recv()
+        turn(1, h)
     rs_opposite(1)
     rs_direct(1)
     w_last(2)

time: 150 us -> 149 us (level)
  no operation moved by 1% of the time
where the time goes in v5:
time: 149 us
  Pallas kernels  147 us (99%)
  local copies, waits for them, and re-layouts  1.74 us (1%)
    pallas_call x1, Pallas kernels, shards(): pl.pallas_call(kernel, out_shape=jax.ShapeDtypeStruct((2 * F, TB), BF16),...  147 us

profile of v5, /device:TPU:1, one launch (start us, length us, event | category | flops | bytes accessed | tf_op | source)
XLA Modules:
  0.0 149.3 jit_solution(25204922134386165)
XLA Ops:
  0.6 146.9 %shard_map.95 = bf16[640,256]{1,0:T(8,128)(2,1)} custom-call(bf16[320,256]{1,0:T(8,128)(2,1)} %bitcast.9, bf16[320,256]{1,0:T(8,128)(2,1)} %bitcast.10, bf16[320,256]{1,0:T(8,128)(2,1)} %wq_ref.1, bf16[320,256]{1,0:T(8,128)(2,1)} %wk_ref.1, bf16[320,256]{1,0:T(8,128)(2,1)} %wv_ref.1, f32[1,256]{1,0:T(1,128)} %bitcast.12, f32[1,256]{1,0:T(1,128)} %bitcast.13, ...), custom_call_target="tpu_custom_call" | custom-call | tf_op jit(solution)/shard_map/pallas_call | solution.py:606
  147.6 1.7 %slice_bitcast_fusion = (bf16[256,320]{0,1:T(8,128)(2,1)}, bf16[256,320]{0,1:T(8,128)(2,1)}) fusion(bf16[640,256]{1,0:T(8,128)(2,1)} %shard_map.95), kind=kLoop, calls=%fused_computation | loop fusion | bytes 655360 | tf_op jit(solution)/shard_map/transpose | solution.py:648

commit v6 on v5

--- a/solution.py
+++ b/solution.py
@@ -518,41 +518,41 @@
     w_last(2)
     w_relay(1)
     wo_send_x(zh)
+    wait(w_sib[2])
+    rs_opposite(4)
+    rs_direct(4)
+    rs_opposite(5)
+    rs_summed(1)
+    keys_out(0)
+    rs_direct(5)
+    w_last(1)
     wait(wo_z)
     wo_send_x(zf)
     wo_send_x(zr)
-    wait(w_sib[2])
-    rs_opposite(4)
-    rs_summed(1)
-    rs_direct(4)
-    keys_out(0)
-    rs_own(1)
-    rs_opposite(5)
-    w_last(1)
-    rs_summed(4)
-    rs_direct(5)
-    keys_out(1)
     wait(w_sib[1])
     rs_opposite(2)
+    rs_own(1)
+    rs_summed(4)
+    rs_direct(2)
+    keys_out(1)
+    rs_opposite(3)
+    rs_own(4)
+    rs_own(5)
+    rs_summed(5)
+    rs_direct(3)
     g_relay(0, 0)
-    rs_own(4)
-    rs_summed(5)
-    rs_direct(2)
+    values_out(0)
     g_relay(0, 1)
-    values_out(0)
-    rs_own(5)
-    rs_opposite(3)
     rs_own(2)
     rs_own(3)
+    rs_summed(2)
     g_last(0, 0)
     g_last(0, 1)
-    for n in range(3):
-        wo_relay_x(n)
-    rs_summed(2)
-    rs_direct(3)
     values_out(1)
     g_relay(1, 0)
     rs_summed(3)
+    for n in range(3):
+        wo_relay_x(n)
     wo_zopp = wo_relay_z()
     g_last(1, 0)
     g_relay(1, 1)

time: 149 us -> 153 us (1.027)
  Pallas kernels: 147 us -> 150 us
    pallas_call x1, Pallas kernels: 147 us -> 150 us  [shards(): pl.pallas_call(kernel, out_shape=jax.ShapeDtypeStruct((2 * F, TB), BF16),...]
where the time goes in v6:
time: 153 us; the launch traced here: 152 us
  Pallas kernels  150 us (98%)
  local copies, waits for them, and re-layouts  1.74 us (1%)
    pallas_call x1, Pallas kernels, shards(): pl.pallas_call(kernel, out_shape=jax.ShapeDtypeStruct((2 * F, TB), BF16),...  150 us

profile of v6, /device:TPU:1, one launch (start us, length us, event | category | flops | bytes accessed | tf_op | source)
XLA Modules:
  0.0 152.5 jit_solution(13130899599022077453)
XLA Ops:
  0.6 150.1 %shard_map.95 = bf16[640,256]{1,0:T(8,128)(2,1)} custom-call(bf16[320,256]{1,0:T(8,128)(2,1)} %bitcast.9, bf16[320,256]{1,0:T(8,128)(2,1)} %bitcast.10, bf16[320,256]{1,0:T(8,128)(2,1)} %wq_ref.1, bf16[320,256]{1,0:T(8,128)(2,1)} %wk_ref.1, bf16[320,256]{1,0:T(8,128)(2,1)} %wv_ref.1, f32[1,256]{1,0:T(1,128)} %bitcast.12, f32[1,256]{1,0:T(1,128)} %bitcast.13, ...), custom_call_target="tpu_custom_call" | custom-call | tf_op jit(solution)/shard_map/pallas_call | solution.py:606
  150.7 1.7 %slice_bitcast_fusion = (bf16[256,320]{0,1:T(8,128)(2,1)}, bf16[256,320]{0,1:T(8,128)(2,1)}) fusion(bf16[640,256]{1,0:T(8,128)(2,1)} %shard_map.95), kind=kLoop, calls=%fused_computation | loop fusion | bytes 655360 | tf_op jit(solution)/shard_map/transpose | solution.py:648

commit v7 on v5

--- a/solution.py
+++ b/solution.py
@@ -131,6 +131,9 @@
             send(ref, AB.at[lax.div(y, 2), half_rows(x, k % 2), cols_of(k // 2)], a_to)
         )
 
+    w_start(0)
+    w_sib[0].append(same(GB.at[c], sibling))
+
     a_own, a_pair, a_two, a_own_opp, a_two_opp = [], [], [], [], []
 
     def a_start(k):
@@ -153,13 +156,13 @@
     a_start(0)
     a_start(1)
     wo_perm = send(wo_ref, WOB.at[wo_row], wo_to)
-    w_start(0)
-    w_sib[0].append(same(GB.at[c], sibling))
+    w_relay(0)
     a_start(2)
     a_own_opp.append(a_relay(nz, a_own, 0))
     a_start(3)
+    w_last(0)
+    w_start(2)
     a_own_opp.append(a_relay(nz, a_own, 1))
-    w_relay(0)
     a_own_opp.append(a_relay(nz, a_own, 2))
     a_own_opp.append(a_relay(nz, a_own, 3))
     for k in range(4):
@@ -177,10 +180,8 @@
             same(wo_half(wo_block(zr, x), 1), z_left),
         ]
 
-    w_start(2)
     wo_perm.wait_recv()
     wo_z = wo_start_z()
-    w_last(0)
 
     wo_x = []
 

time: 149 us -> 154 us (1.034)
  Pallas kernels: 147 us -> 151 us
    pallas_call x1, Pallas kernels: 147 us -> 151 us  [shards(): pl.pallas_call(kernel, out_shape=jax.ShapeDtypeStruct((2 * F, TB), BF16),...]
where the time goes in v7:
time: 154 us; the launch traced here: 153 us
  Pallas kernels  151 us (98%)
  local copies, waits for them, and re-layouts  1.74 us (1%)
    pallas_call x1, Pallas kernels, shards(): pl.pallas_call(kernel, out_shape=jax.ShapeDtypeStruct((2 * F, TB), BF16),...  151 us

profile of v7, /device:TPU:1, one launch (start us, length us, event | category | flops | bytes accessed | tf_op | source)
XLA Modules:
  0.0 153.4 jit_solution(14142709892022662661)
XLA Ops:
  0.6 151.0 %shard_map.95 = bf16[640,256]{1,0:T(8,128)(2,1)} custom-call(bf16[320,256]{1,0:T(8,128)(2,1)} %bitcast.9, bf16[320,256]{1,0:T(8,128)(2,1)} %bitcast.10, bf16[320,256]{1,0:T(8,128)(2,1)} %wq_ref.1, bf16[320,256]{1,0:T(8,128)(2,1)} %wk_ref.1, bf16[320,256]{1,0:T(8,128)(2,1)} %wv_ref.1, f32[1,256]{1,0:T(1,128)} %bitcast.12, f32[1,256]{1,0:T(1,128)} %bitcast.13, ...), custom_call_target="tpu_custom_call" | custom-call | tf_op jit(solution)/shard_map/pallas_call | solution.py:607
  151.6 1.7 %slice_bitcast_fusion = (bf16[256,320]{0,1:T(8,128)(2,1)}, bf16[256,320]{0,1:T(8,128)(2,1)}) fusion(bf16[640,256]{1,0:T(8,128)(2,1)} %shard_map.95), kind=kLoop, calls=%fused_computation | loop fusion | bytes 655360 | tf_op jit(solution)/shard_map/transpose | solution.py:649

commit v8 on v5

--- a/solution.py
+++ b/solution.py
@@ -152,12 +152,12 @@
 
     a_start(0)
     a_start(1)
-    wo_perm = send(wo_ref, WOB.at[wo_row], wo_to)
-    w_start(0)
-    w_sib[0].append(same(GB.at[c], sibling))
     a_start(2)
     a_own_opp.append(a_relay(nz, a_own, 0))
     a_start(3)
+    w_start(0)
+    w_sib[0].append(same(GB.at[c], sibling))
+    wo_perm = send(wo_ref, WOB.at[wo_row], wo_to)
     a_own_opp.append(a_relay(nz, a_own, 1))
     w_relay(0)
     a_own_opp.append(a_relay(nz, a_own, 2))

time: 149 us -> 151 us (1.013)
  no operation moved by 1% of the time
where the time goes in v8:
time: 151 us
  Pallas kernels  148 us (98%)
  local copies, waits for them, and re-layouts  1.74 us (1%)
    pallas_call x1, Pallas kernels, shards(): pl.pallas_call(kernel, out_shape=jax.ShapeDtypeStruct((2 * F, TB), BF16),...  148 us

profile of v8, /device:TPU:1, one launch (start us, length us, event | category | flops | bytes accessed | tf_op | source)
XLA Modules:
  0.0 150.5 jit_solution(10560911163175131754)
XLA Ops:
  0.6 148.2 %shard_map.95 = bf16[640,256]{1,0:T(8,128)(2,1)} custom-call(bf16[320,256]{1,0:T(8,128)(2,1)} %bitcast.9, bf16[320,256]{1,0:T(8,128)(2,1)} %bitcast.10, bf16[320,256]{1,0:T(8,128)(2,1)} %wq_ref.1, bf16[320,256]{1,0:T(8,128)(2,1)} %wk_ref.1, bf16[320,256]{1,0:T(8,128)(2,1)} %wv_ref.1, f32[1,256]{1,0:T(1,128)} %bitcast.12, f32[1,256]{1,0:T(1,128)} %bitcast.13, ...), custom_call_target="tpu_custom_call" | custom-call | tf_op jit(solution)/shard_map/pallas_call | solution.py:606
  148.8 1.7 %slice_bitcast_fusion = (bf16[256,320]{0,1:T(8,128)(2,1)}, bf16[256,320]{0,1:T(8,128)(2,1)}) fusion(bf16[640,256]{1,0:T(8,128)(2,1)} %shard_map.95), kind=kLoop, calls=%fused_computation | loop fusion | bytes 655360 | tf_op jit(solution)/shard_map/transpose | solution.py:648
